TPU v7x, 128 devices: a whole 4x4x4 slice. The times are simulated.
128 devices in a mesh: prow: 8 (over x, core), pcol: 16 (over y, z).
Axes of the slice: x: 4, y: 4, z: 4, core: 2. Of those that a mesh axis runs over, the one named last changes fastest.
Arguments:
- front: float32 [59, 8, 128, 1, 16, 128], P(None, 'prow', None, None, 'pcol'), may hold values from -66 to 396
- child: float32 [2, 8, 8, 128, 16, 128], P(None, None, 'prow', None, 'pcol'), may hold values from -6 to 6
- row_map: int32 [2, 64], replicated, may hold values from 0 to 471, as said below
- col_map: int32 [2, 16], replicated, may hold values from 0 to 15, as said below
Outputs:
- factor: float32 [59, 8, 128, 1, 16, 128], P(None, 'prow', None, None, 'pcol')
Inputs may be any that keep to these rules, and one draw needn't show every extreme that they name: Within one child all entries differ. For each child c and each index p of prow, the entries row_map[c, l * 8 + p] for l = 0 .. 7 have different remainders modulo 8. `col_map`: within one child all entries differ.
All inputs are finite; a program needn't handle non-finite values.
Results may differ from a plain program's by a relative error of at most 0.0001.
Values sent between devices are 32-bit elements; how exact they have to be, the bound alone decides.
No kernel may reach another device: no remote copies, remote signals or barrier semaphores. Data moves between devices by JAX's collectives and lax.ppermute only.
A program may use at most 128 MiB of HBM per device.

v0:
```python
import jax
import jax.numpy as jnp
from jax import lax
from jax.sharding import PartitionSpec as P

HIGHEST_PRECISION = lax.Precision.HIGHEST


def broadcast(block, axis, holder):
    block = jnp.where(lax.axis_index(axis) == holder, block, jnp.zeros_like(block))
    return lax.psum(block, axis)


def spread(strip, root):
    return broadcast(strip, "pcol", root)


def sort_by_owner(blocks, owners, prow_count):
    choose = (owners[:, None, :] == jnp.arange(prow_count)[None, :, None]).astype(jnp.float32)
    return jnp.einsum("cdl,clrx->cdrx", choose, blocks, precision=HIGHEST_PRECISION)


def place_columns(carry, piece, col_map, col_here, pcol_count, block_size):
    count = piece.shape[3] // block_size
    target = jnp.arange(carry.shape[3]) * pcol_count + col_here
    pick = (col_map[:, :, None] == target[None, None, :]).astype(jnp.float32)
    shaped = piece.reshape(piece.shape[0], piece.shape[1], block_size, count, block_size)
    return jnp.einsum("csrtk,ctm->csrmk", shaped, pick, precision=HIGHEST_PRECISION)


def on_device(front, child, row_map, col_map):
    row_blocks = front.shape[0]
    block_size = front.shape[2]
    col_blocks = front.shape[3]
    prow_count = lax.axis_size("prow")
    pcol_count = lax.axis_size("pcol")
    row_here = lax.axis_index("prow")
    col_here = lax.axis_index("pcol")
    local_rows = child.shape[1]
    matrix = front.reshape(row_blocks * block_size, col_blocks * block_size)
    table = row_map.reshape(2, local_rows, prow_count)
    owners = (
        jnp.sum(jnp.where(jnp.arange(prow_count)[None, None, :] == row_here, table, 0), axis=2)
        % prow_count
    )
    arrival = jnp.sum(jnp.where(table % prow_count == row_here, table // prow_count, 0), axis=1)
    raw = child.reshape(2, local_rows, block_size, block_size)
    moved = lax.all_to_all(
        sort_by_owner(raw, owners, prow_count), "prow", split_axis=1, concat_axis=1, tiled=True
    )
    empty = jnp.zeros((2, prow_count, block_size, col_blocks, block_size), jnp.float32)
    placed = place_columns(
        empty,
        lax.all_gather(moved, "pcol", axis=3, tiled=True),
        col_map,
        col_here,
        pcol_count,
        block_size,
    )
    arrived = placed.reshape(2, prow_count, block_size, col_blocks * block_size)
    stacked = matrix.reshape(row_blocks, block_size, col_blocks * block_size)
    for member in range(2):
        stacked = stacked.at[arrival[member]].add(arrived[member])
    matrix = stacked.reshape(row_blocks * block_size, col_blocks * block_size)
    row_ids = (
        (jnp.arange(row_blocks)[:, None] * prow_count + row_here) * block_size
        + jnp.arange(block_size)[None, :]
    ).reshape(-1)
    col_ids = (
        (jnp.arange(col_blocks)[:, None] * pcol_count + col_here) * block_size
        + jnp.arange(block_size)[None, :]
    ).reshape(-1)
    for segment in range(2):
        start_col = 2 * segment * block_size
        stop_col = start_col + 2 * block_size
        strips = [spread(matrix, 2 * segment + member) for member in range(2)]
        panel = jnp.concatenate(strips, axis=1)
        wanted = [jnp.int32(2 * segment), jnp.int32(2 * segment + 1)]
        wanted = wanted + [col_here + 0]
        pieces = []
        for target in wanted:
            section = lax.dynamic_slice_in_dim(
                panel, target // prow_count * block_size, block_size, 0
            )
            pieces.append(jnp.where(target % prow_count == row_here, section, 0.0))
        gathered = lax.psum(jnp.concatenate(pieces, axis=0), "prow")
        diag = gathered[: 2 * block_size]
        sym = jnp.tril(diag) + jnp.tril(diag, -1).T
        lower = jnp.linalg.cholesky(sym)
        inverse = lax.linalg.triangular_solve(
            lower, jnp.eye(2 * block_size, dtype=jnp.float32), left_side=True, lower=True
        )
        factor = jnp.dot(panel, inverse.T, precision=HIGHEST_PRECISION)
        col_factor = jnp.dot(gathered[2 * block_size :], inverse.T, precision=HIGHEST_PRECISION)
        shaped = factor.reshape(row_blocks, block_size, 2 * block_size)
        for member in range(2):
            target = 2 * segment + member
            slot = target // prow_count
            replaced = jnp.where(
                row_here == target % prow_count,
                lower[member * block_size : (member + 1) * block_size],
                shaped[slot],
            )
            shaped = shaped.at[slot].set(replaced)
        factor = shaped.reshape(row_blocks * block_size, 2 * block_size)
        for member in range(2):
            owned = col_here == 2 * segment + member
            written = jnp.where(
                owned, factor[:, member * block_size : (member + 1) * block_size], matrix
            )
            matrix = matrix.at[:, :block_size].set(written)
        change = jnp.dot(factor, col_factor.T, precision=HIGHEST_PRECISION)
        matrix = matrix - jnp.where(col_ids[None, :] >= stop_col, change, 0.0)
    keep = row_ids[:, None] >= jnp.minimum(col_ids, 4 * block_size)[None, :]
    return jnp.where(keep, matrix, 0.0).reshape(front.shape)


def solution(mesh):
    return jax.shard_map(
        on_device,
        mesh=mesh,
        in_specs=(
            P(None, "prow", None, None, "pcol", None),
            P(None, None, "prow", None, "pcol", None),
            P(),
            P(),
        ),
        out_specs=P(None, "prow", None, None, "pcol", None),
        check_vma=False,
    )
```

profile of v0, /device:TPU:0, one launch (start us, length us, event | category | flops | bytes accessed | tf_op | source)
XLA Modules:
  0.0 761.4 jit_solution(10043648452690605606)
XLA Ops:
  6.5 4.5 copy.75
  11.4 1.2 fusion.7
  12.7 20.4 %all_to_all.5 = f32[2,8,128,128]{3,2,0,1:T(8,128)} all-to-all(f32[2,8,128,128]{3,2,0,1:T(8,128)S(1)} %copy.14), channel_id=1, replica_groups=mesh['prow'=8,'pcol'=16] {'prow'}, dimensions={1} | all-to-all | bytes 2097152 | tf_op jit(solution)/shard_map/all_to_all | solution.py:48
  33.2 121.8 %all-gather.2.cloned.1.call-done = f32[2,8,128,2048]{3,2,0,1:T(8,128)} async-done(((f32[2,8,128,128]{3,2,0,1:T(8,128)}), f32[2,8,128,2048]{3,2,0,1:T(8,128)}) %all-gather.2.cloned.1.call-update) | async-done | bytes 16777232 | tf_op jit(solution)/shard_map/all_gather | solution.py:54
  155.0 9.4 %copy.32 = f32[256,8,16,128]{3,2,1,0:T(8,128)S(1)} copy(f32[256,8,16,128]{3,1,2,0:T(8,128)} %bitcast.134) | data formatting | bytes 33554432
  164.4 6.5 fusion
  171.0 2.7 scatter_fusion
  173.7 2.7 scatter_fusion.1
  176.4 5.7 bitcast_select_fusion
  182.2 134.7 %all-reduce.14.cloned.1.call-done = (f32[7552,128]{1,0:T(8,128)}, f32[7552,128]{1,0:T(8,128)}) async-done(((f32[7552,128]{1,0:T(8,128)}, f32[7552,128]{1,0:T(8,128)}), (f32[7552,128]{1,0:T(8,128)}, f32[7552,128]{1,0:T(8,128)})) %all-reduce.14.cloned.1.call-update) | async-done | bytes 7733264 | tf_op jit(solution)/shard_map/psum | solution.py:11
  316.9 2.5 constant_dynamic-update-slice_fusion.1
  319.5 0.7 copy-done.6
  320.2 0.3 constant_dynamic-update-slice_fusion
  320.5 3.0 copy-done.3
  323.6 0.8 pad_maximum_fusion
  324.7 59.9 %all-reduce.8.cloned.1.call-done = f32[384,256]{1,0:T(8,128)} async-done(((f32[384,256]{1,0:T(8,128)}), f32[384,256]{1,0:T(8,128)}) %all-reduce.8.cloned.1.call-update) | async-done | bytes 393232 | tf_op jit(solution)/shard_map/psum | solution.py:86
  384.6 1.0 slice.289
  385.7 1.0 bitcast_add_fusion.3
  387.0 11.7 %cholesky.130 = f32[128,128]{1,0:T(8,128)S(1)} custom-call(f32[128,128]{1,0:T(8,128)S(1)} %cholesky.194), custom_call_target="Cholesky" | custom-call | tf_op jit(solution)/shard_map/jit(cholesky)/cholesky | solution.py:89
  398.7 9.8 %custom-call.13 = f32[1,128,128]{1,2,0:T(8,128)S(1)} custom-call(f32[1,128,128]{2,1,0:T(8,128)S(1)} %get-tuple-element.200), custom_call_target="InvertDiagBlocksLowerTriangular" | custom-call | tf_op jit(solution)/shard_map/jit(cholesky)/cholesky | solution.py:89
  408.8 0.3 convolution_subtract_fusion.3
  409.0 11.7 %cholesky.147 = f32[128,128]{1,0:T(8,128)S(1)} custom-call(f32[128,128]{1,0:T(8,128)S(1)} %convolution_subtract_fusion.3), custom_call_target="Cholesky" | custom-call | tf_op jit(solution)/shard_map/jit(cholesky)/cholesky | solution.py:89
  420.8 0.7 compare_reduce_fusion.2
  422.9 4.3 while.16
  423.1 0.7 fusion.77
  423.8 1.4 bitcast_dynamic-update-slice_fusion.6
  425.2 0.7 fusion.77
  425.8 1.4 bitcast_dynamic-update-slice_fusion.6
  427.2 19.7 %custom-call.14 = f32[2,128,128]{1,2,0:T(8,128)S(1)} custom-call(f32[2,128,128]{2,1,0:T(8,128)S(1)} %get-tuple-element.149), custom_call_target="InvertDiagBlocksLowerTriangular" | custom-call | tf_op jit(solution)/shard_map/triangular_solve/custom-call.0 | solution.py:90
  446.9 0.3 fusion.27
  447.5 0.3 fusion.34
  447.8 9.0 %fusion.18 = f32[7552,256]{1,0:T(8,128)S(1)} fusion(f32[7552,256]{1,0:T(8,128)} %copy-done.3, f32[128,256]{1,0:T(8,128)S(1)} %fusion.34, f32[128,256]{1,0:T(8,128)S(1)} %fusion.27), kind=kOutput, calls=%fused_computation.52 | convolution fusion | flops 5939200000 | bytes 15728640 | tf_op jit(solution)/shard_map/dot_general | solution.py:93
  456.8 0.9 copy.55
  457.7 1.5 fusion.17
  459.2 9.2 %broadcast_select_fusion = (f32[7552,128]{1,0:T(8,128)}, f32[7552,128]{1,0:T(8,128)}, f32[7552,128]{1,0:T(8,128)}) fusion(pred[]{:T(512)S(6)} %eq.100, pred[]{:T(512)S(6)} %eq.101, f32[7552,256]{1,0:T(8,128)S(1)} %bitcast.132, f32[128,256]{1,0:T(8,128)S(1)} %fusion.17, pred[128]{0:T(512)(128)(4,1)S(1)} %fusion.52, f32[7552,128]{1,0:T(8,128)S(1)} %bitcast.131, ...), kind=kOutput, calls=%fused_computation.19 | convolution fusion | flops 2975367168 | bytes 31064580 | tf_op jit(solution)/shard_map/dot_general | solution.py:112
  468.4 0.4 all-reduce.10.cloned.1.call-start
  469.2 134.1 %all-reduce.12.cloned.1.call-done = (f32[7552,128]{1,0:T(8,128)}, f32[7552,128]{1,0:T(8,128)}) async-done(((f32[7552,128]{1,0:T(8,128)}, f32[7552,128]{1,0:T(8,128)}), (f32[7552,128]{1,0:T(8,128)}, f32[7552,128]{1,0:T(8,128)})) %all-reduce.12.cloned.1.call-update) | async-done | bytes 7733264 | tf_op jit(solution)/shard_map/psum | solution.py:11
  603.3 2.5 constant_dynamic-update-slice_fusion.3
  605.8 0.7 copy-done.7
  606.5 0.3 constant_dynamic-update-slice_fusion.2
  606.8 3.0 copy-done.4
  609.9 0.8 pad_maximum_fusion.1
  610.8 60.1 %all-reduce.10.cloned.1.call-done = f32[384,256]{1,0:T(8,128)} async-done(((f32[384,256]{1,0:T(8,128)}), f32[384,256]{1,0:T(8,128)}) %all-reduce.10.cloned.1.call-update) | async-done | bytes 393232 | tf_op jit(solution)/shard_map/psum | solution.py:86
  670.9 1.0 slice_select_fusion.2
  672.0 1.0 bitcast_add_fusion.1
  673.3 11.7 %cholesky.164 = f32[128,128]{1,0:T(8,128)S(1)} custom-call(f32[128,128]{1,0:T(8,128)S(1)} %cholesky.197), custom_call_target="Cholesky" | custom-call | tf_op jit(solution)/shard_map/jit(cholesky)/cholesky | solution.py:89
  685.0 9.8 %custom-call.15 = f32[1,128,128]{1,2,0:T(8,128)S(1)} custom-call(f32[1,128,128]{2,1,0:T(8,128)S(1)} %get-tuple-element.196), custom_call_target="InvertDiagBlocksLowerTriangular" | custom-call | tf_op jit(solution)/shard_map/jit(cholesky)/cholesky | solution.py:89
  695.1 0.3 convolution_subtract_fusion.2
  695.3 11.7 %cholesky.181 = f32[128,128]{1,0:T(8,128)S(1)} custom-call(f32[128,128]{1,0:T(8,128)S(1)} %convolution_subtract_fusion.2), custom_call_target="Cholesky" | custom-call | tf_op jit(solution)/shard_map/jit(cholesky)/cholesky | solution.py:89
  707.1 0.7 compare_reduce_fusion
  707.8 0.6 compare_reduce_fusion.1
  709.9 4.3 while.17
  710.1 0.6 fusion.78
  710.7 1.4 bitcast_dynamic-update-slice_fusion.7
  712.1 0.6 fusion.78
  712.7 1.4 bitcast_dynamic-update-slice_fusion.7
  714.1 19.7 %custom-call.16 = f32[2,128,128]{1,2,0:T(8,128)S(1)} custom-call(f32[2,128,128]{2,1,0:T(8,128)S(1)} %get-tuple-element.150), custom_call_target="InvertDiagBlocksLowerTriangular" | custom-call | tf_op jit(solution)/shard_map/triangular_solve/custom-call.0 | solution.py:90
  733.8 0.3 fusion.25
  734.1 0.3 convolution_subtract_fusion
  734.4 0.3 fusion.30
  734.7 8.5 %fusion.16 = f32[7552,256]{1,0:T(8,128)S(1)} fusion(f32[7552,256]{1,0:T(8,128)} %copy-done.4, f32[128,256]{1,0:T(8,128)S(1)} %fusion.30, f32[128,256]{1,0:T(8,128)S(1)} %fusion.25), kind=kOutput, calls=%fused_computation.50 | convolution fusion | flops 5939200000 | bytes 15728640 | tf_op jit(solution)/shard_map/dot_general | solution.py:93
  743.3 0.9 copy.69
  744.3 1.5 fusion.15
  745.8 8.9 %fusion.4 = f32[7552,128]{1,0:T(8,128)} fusion(f32[7552,256]{1,0:T(8,128)S(1)} %bitcast.133, f32[128,256]{1,0:T(8,128)S(1)} %fusion.15, f32[7552,128]{1,0:T(8,128)S(1)} %copy-done.5, s32[128]{0:T(128)S(1)} %fusion.53, s32[7552]{0:T(1024)S(1)} %add_bitcast_fusion, pred[128]{0:T(512)(128)(4,1)S(1)} %fusion.51, pred[]{:T(512)S(6)} %eq.101, pred[]{:T(512)S(6)} %eq.100), kind=kOutput, calls=%fused_computation.12 | convolution fusion | flops 2975367168 | bytes 23364610 | tf_op jit(solution)/shard_map/dot_general | solution.py:112
  (75 shorter events, 3.1 us)
Async XLA Ops:
  6.5 4.8 copy-start
  6.5 4.6 copy-start.8
  6.5 26.7 %copy-start.9 = (s32[2,16]{1,0:T(2,128)S(1)}, s32[2,16]{1,0:T(2,128)}, u32[]{:S(2)}) copy-start(s32[2,16]{1,0:T(2,128)} %param.34) | copy-start | bytes 388
  6.5 148.5 %all-gather.2.cloned.1.call-start = ((), (), s32[]{:S(2)}) async-start(), calls=%async_computation.1 | async-start | bytes 17825792 | tf_op jit(solution)/shard_map/all_gather | solution.py:54
  33.2 283.8 %all-reduce.14.cloned.1.call-start = ((), (), s32[]{:S(2)}) async-start(), calls=%async_computation.5 | async-start | bytes 15466496 | tf_op jit(solution)/shard_map/psum | solution.py:11
  182.1 202.5 %all-reduce.8.cloned.1.call-start = ((), (), s32[]{:S(2)}) async-start(), calls=%async_computation.2 | async-start | bytes 786432 | tf_op jit(solution)/shard_map/psum | solution.py:86
  316.9 3.3 copy-start.6
  320.5 3.1 copy-start.3
  324.4 278.9 %all-reduce.12.cloned.1.call-start = ((), (), s32[]{:S(2)}) async-start(), calls=%async_computation.4 | async-start | bytes 15466496 | tf_op jit(solution)/shard_map/psum | solution.py:11
  456.8 2.5 copy-start.2
  468.4 202.5 %all-reduce.10.cloned.1.call-start = ((), (), s32[]{:S(2)}) async-start(), calls=%async_computation.3 | async-start | bytes 786432 | tf_op jit(solution)/shard_map/psum | solution.py:86
  603.3 3.3 copy-start.7
  606.8 3.1 copy-start.4
  743.3 2.5 copy-start.5
  745.7 9.0 %copy-start.1 = (f32[2,8,1,128,1,128]{5,4,3,2,1,0:T(1,128)S(1)}, f32[2,8,1,128,1,128]{5,4,3,2,1,0:T(1,128)}, u32[]{:S(2)}) copy-start(f32[2,8,1,128,1,128]{5,4,3,2,1,0:T(1,128)} %param.32) | copy-start | bytes 3145732
Sparse Core Ops, SparseCore 0:
  33.3 121.7 all-gather.1
  182.2 134.6 all-reduce.13
  324.5 60.0 all-reduce.7
  468.6 134.6 all-reduce.11
  610.8 60.0 all-reduce.9
where the time goes:
time: 769 us; the launch traced here: 761 us
  waiting for transfers between devices  511 us (66%)
  other arithmetic  124 us (16%)
  matrix products  49 us (6%)
  local copies, waits for them, and re-layouts  39.2 us (5%)
  blocking collectives  20.4 us (3%)
  between operations  16.6 us (2%)
    psum x2, waiting for transfers between devices, broadcast(): return lax.psum(block, axis)  269 us
    all_gather x1, waiting for transfers between devices, on_device(): lax.all_gather(moved, 'pcol', axis=3, tiled=True)  122 us
    psum x2, waiting for transfers between devices, on_device(): gathered = lax.psum(jnp.concatenate(pieces, axis=0), 'prow')  120 us
    another operation x13, other arithmetic, on_device(): lower = jnp.linalg.cholesky(sym)  68.7 us
    another operation x5, other arithmetic, on_device(): lax.linalg.triangular_solve(lower, jnp.eye(2 * block_size, dtype=jnp.floa...  39.4 us
    unnamed x26, local copies, waits for them, and re-layouts  28.4 us
    all_to_all x1, blocking collectives, on_device(): lax.all_to_all(sort_by_owner(raw, owners, prow_count), 'prow', split_axis...  20.4 us
    dot_general x2, matrix products, on_device(): change = jnp.dot(factor, col_factor.T, precision=HIGHEST_PRECISION)  18.1 us
  transfers between devices with their start and end apart: 5, of which 5 were waited for; matrix products, arithmetic and copies ran while one was open for 0% of the time, Pallas kernels for 0%

commit v1 on v0

v1 whole, which is shorter than its diff:
```python
import functools

import jax
import jax.numpy as jnp
from jax import lax
from jax.experimental import pallas as pl
from jax.experimental.pallas import tpu as pltpu
from jax.sharding import PartitionSpec as P

BS = 128
TOP = 4
PROWS = 8
PCOLS = 16
SUB = 32
GROUP = 4
BOTH = ("prow", "pcol")
NN = (((1,), (0,)), ((), ()))
NT = (((1,), (1,)), ((), ()))
TN = (((0,), (0,)), ((), ()))
VMEM_LIMIT = 48 << 20


def vmem():
    return pl.BlockSpec(memory_space=pltpu.VMEM)


def smem():
    return pl.BlockSpec(memory_space=pltpu.SMEM)


def params():
    return pltpu.CompilerParams(vmem_limit_bytes=VMEM_LIMIT)


def exact_dot(a, b, dims=NN):
    return lax.dot_general(
        a, b, dims, precision=lax.Precision.HIGHEST, preferred_element_type=jnp.float32
    )


def route_kernel(col_ref, table_ref, got_ref, onward_ref, top_ref, inverse, pack):
    for c in range(2):
        for q in range(PCOLS):
            inverse[c, col_ref[c, q]] = q
    out_id = lax.broadcasted_iota(jnp.int32, (64, 64), 0)
    in_id = lax.broadcasted_iota(jnp.int32, (64, 64), 1)
    wanted = lax.broadcasted_iota(jnp.int32, (16, 64), 0)
    sums = [
        jnp.concatenate([got_ref[:, k, 16 + s, :] for s in range(2)], axis=0)
        for k in range(TOP)
    ]
    for c in range(2):
        table = table_ref[c : c + 1, :]
        move = (out_id % 8 == in_id // 8) & (out_id // 8 == jnp.broadcast_to(table, (64, 64)) % 8)
        move = move.astype(jnp.float32)
        pick = (wanted == jnp.broadcast_to(table, (16, 64))).astype(jnp.float32)
        for q in range(PCOLS):
            source = inverse[c, q]
            rows = got_ref[:, source, 8 * c : 8 * c + 8, :].reshape(64, BS)
            onward_ref[:, q, 8 * c : 8 * c + 8, :] = exact_dot(move, rows).reshape(8, 8, BS)
            if q < TOP:
                sums[q] = sums[q] + exact_dot(pick, rows)
    pack[...] = jnp.zeros_like(pack)
    place = 0
    for t in range(TOP):
        for k in range(t + 1):
            pack[place : place + 1, :] = sums[k][t : t + 1, :]
            place += 1
    for q in range(PCOLS):
        for k in range(TOP):
            pack[place + k : place + k + 1, :] = sums[k][q : q + 1, :]
        top_ref[:, q] = jnp.broadcast_to(pack[...][None], (PROWS, 16, BS))


def route(col_map, table, got):
    return pl.pallas_call(
        route_kernel,
        out_shape=(
            jax.ShapeDtypeStruct((PROWS, PCOLS, 16, BS), jnp.float32),
            jax.ShapeDtypeStruct((PROWS, PCOLS, 16, BS), jnp.float32),
        ),
        in_specs=[smem(), vmem(), vmem()],
        out_specs=[vmem(), vmem()],
        scratch_shapes=[pltpu.SMEM((2, PCOLS), jnp.int32), pltpu.VMEM((16, BS), jnp.float32)],
        compiler_params=params(),
        name="route",
    )(col_map, table, got)


def factor_block(tab, up, width):
    for k0 in range(0, BS, width):
        rows = [jnp.broadcast_to(tab[k0 + i : k0 + i + 1, :], (8, 2 * BS)) for i in range(width)]
        a = [
            [jnp.broadcast_to(rows[i][:, k0 + j : k0 + j + 1], (8, BS)) for j in range(i + 1)]
            for i in range(width)
        ]
        scale = [None] * width
        for j in range(width):
            scale[j] = lax.rsqrt(a[j][j])
            for i in range(j + 1, width):
                a[i][j] = a[i][j] * scale[j]
            for i in range(j + 1, width):
                for m in range(j + 1, i + 1):
                    a[i][m] = a[i][m] - a[i][j] * a[m][j]
        done = []
        for i in range(width):
            halves = []
            for h in range(2):
                u = rows[i][:, h * BS : (h + 1) * BS]
                for j in range(i):
                    u = u - a[i][j] * done[j][h]
                halves.append(u * scale[i])
            done.append(halves)
            up[k0 + i : k0 + i + 1, 0:BS] = halves[0][0:1]
            up[k0 + i : k0 + i + 1, BS:] = halves[1][0:1]
        after = k0 + width
        if after < BS:
            panel = up[k0:after, :]
            tab[after:, :] = tab[after:, :] - exact_dot(panel[:, :BS], panel, TN)[after:, :]


def cholesky_kernel(width, place_ref, got_ref, weight_ref, top_ref, work, low, tab, up, inverses):
    row = lax.broadcasted_iota(jnp.int32, (BS, BS), 0)
    col = lax.broadcasted_iota(jnp.int32, (BS, BS), 1)
    eye = (row == col).astype(jnp.float32)
    place = 0
    for t in range(TOP):
        for k in range(t + 1):
            work[t * BS : (t + 1) * BS, k * BS : (k + 1) * BS] = got_ref[:, place, :]
            place += 1
    for k in range(TOP):
        work[TOP * BS :, k * BS : (k + 1) * BS] = got_ref[:, place + k, :]
    low[...] = jnp.zeros_like(low)
    for k in range(TOP):
        lo, hi = k * BS, (k + 1) * BS
        block = work[lo:hi, lo:hi]
        tab[:, :BS] = jnp.where(row >= col, block, block.T)
        tab[:, BS:] = eye
        factor_block(tab, up, width)
        low[lo:hi, lo:hi] = jnp.where(row >= col, up[:, :BS].T, 0.0)
        inverse = up[:, BS:]
        inverses[lo:hi, :] = inverse
        below = exact_dot(work[hi:, lo:hi], inverse, NT)
        work[hi:, lo:hi] = below
        if k + 1 < TOP:
            count = (TOP - 1 - k) * BS
            low[hi:, lo:hi] = below[:count]
            work[hi:, hi:] = work[hi:, hi:] - exact_dot(below, below[:count], NT)
    my_row = place_ref[0]
    my_col = place_ref[1]
    for k in reversed(range(TOP)):
        lo, hi = k * BS, (k + 1) * BS
        solved = work[TOP * BS :, lo:hi].T
        rhs = jnp.where(my_col >= TOP, solved, jnp.where(my_col == k, -eye, 0.0))
        if k + 1 < TOP:
            rhs = rhs - exact_dot(work[hi : TOP * BS, lo:hi], weight_ref[hi:, :], TN)
        weight_ref[lo:hi, :] = exact_dot(inverses[lo:hi, :], rhs, TN)
    r0 = pl.multiple_of(jnp.minimum(my_row, TOP - 1) * BS, BS)
    c0 = pl.multiple_of(jnp.minimum(my_col, TOP - 1) * BS, BS)
    top_ref[...] = jnp.where(my_col < TOP, low[pl.ds(r0, BS), pl.ds(c0, BS)], 0.0)


def cholesky(place, got):
    return pl.pallas_call(
        functools.partial(cholesky_kernel, 16),
        out_shape=(
            jax.ShapeDtypeStruct((TOP * BS, BS), jnp.float32),
            jax.ShapeDtypeStruct((BS, BS), jnp.float32),
        ),
        in_specs=[smem(), vmem()],
        out_specs=[vmem(), vmem()],
        scratch_shapes=[
            pltpu.VMEM(((TOP + 1) * BS, TOP * BS), jnp.float32),
            pltpu.VMEM((TOP * BS, TOP * BS), jnp.float32),
            pltpu.VMEM((BS, 2 * BS), jnp.float32),
            pltpu.VMEM((BS, 2 * BS), jnp.float32),
            pltpu.VMEM((TOP * BS, BS), jnp.float32),
        ],
        compiler_params=params(),
        name="cholesky",
    )(place, got)


def assemble_kernel(slot_ref, f0, f1, f2, f3, c0, c1, c2, c3, out_ref):
    out_ref[...] = f0[...] + f1[...] + f2[...] + f3[...]
    for i in range(16):
        slot = slot_ref[i]
        out_ref[slot] = out_ref[slot] + (c0[i] + c1[i] + c2[i] + c3[i])


def assemble(slots, front_parts, child_parts):
    return pl.pallas_call(
        assemble_kernel,
        out_shape=jax.ShapeDtypeStruct(front_parts[0].shape, jnp.float32),
        in_specs=[smem()] + [vmem()] * 8,
        out_specs=vmem(),
        compiler_params=params(),
        name="assemble",
    )(slots, *front_parts, *child_parts)


def update_kernel(place_ref, which_ref, weight_ref, top_ref, child_ref, panel_ref, front_ref, out_ref, high, wide):
    step = pl.program_id(0)

    @pl.when(step == 0)
    def _():
        weight = weight_ref[...]
        big = weight.astype(jnp.bfloat16)
        small = (weight - big.astype(jnp.float32)).astype(jnp.bfloat16)
        high[...] = big
        wide[...] = jnp.concatenate([big, small], axis=1)

    rows = GROUP * BS
    parts = []
    for z in range(TOP):
        piece = jnp.stack([panel_ref[4 * y + z] for y in range(4)], axis=1)
        parts.append(piece.reshape(rows, BS))
    panel = jnp.concatenate(parts, axis=1)
    big = panel.astype(jnp.bfloat16)
    small = (panel - big.astype(jnp.float32)).astype(jnp.bfloat16)
    first = lax.dot_general(big, wide[...], NN, preferred_element_type=jnp.float32)
    second = lax.dot_general(small, high[...], NN, preferred_element_type=jnp.float32)
    change = first[:, :BS] + (first[:, BS:] + second)
    base = jnp.where(place_ref[1] >= TOP, front_ref[...], 0.0)
    out_ref[...] = base - change.reshape(GROUP, BS, BS)
    for i in range(GROUP):
        for c in range(2):
            source = which_ref[c, step * GROUP + i]

            @pl.when((source >= 0) & (place_ref[1] >= TOP))
            def _():
                out_ref[i] = out_ref[i] + child_ref[jnp.maximum(source, 0)]

    @pl.when((step == 0) & (place_ref[0] < TOP))
    def _():
        out_ref[0] = top_ref[...]


def update(place, which, weight, top, child, panel, front):
    count = front.shape[0]
    return pl.pallas_call(
        update_kernel,
        out_shape=jax.ShapeDtypeStruct(front.shape, jnp.float32),
        grid=(pl.cdiv(count, GROUP),),
        in_specs=[
            smem(),
            smem(),
            vmem(),
            vmem(),
            vmem(),
            pl.BlockSpec((PCOLS, GROUP, SUB, BS), lambda i: (0, i, 0, 0)),
            pl.BlockSpec((GROUP, BS, BS), lambda i: (i, 0, 0)),
        ],
        out_specs=pl.BlockSpec((GROUP, BS, BS), lambda i: (i, 0, 0)),
        scratch_shapes=[
            pltpu.VMEM((TOP * BS, BS), jnp.bfloat16),
            pltpu.VMEM((TOP * BS, 2 * BS), jnp.bfloat16),
        ],
        compiler_params=params(),
        name="update",
    )(place, which, weight, top, child, panel, front)


def scatter_rows(blocks):
    lane = lax.axis_index("pcol")
    parts = [jnp.where(lane < TOP, blocks[:, :SUB], 0.0)]
    for y in range(1, 4):
        pairs = [(k, 4 * y + k) for k in range(TOP)]
        parts.append(lax.ppermute(blocks[:, y * SUB : (y + 1) * SUB], "pcol", pairs))
    return parts


def on_device(front, child, row_map, col_map):
    count = front.shape[0]
    row_here = lax.axis_index("prow")
    col_here = lax.axis_index("pcol")
    place = jnp.stack([row_here, col_here]).astype(jnp.int32)
    blocks = front.reshape(count, BS, BS)
    pieces = child.reshape(16, BS, BS)
    by_source = row_map.reshape(2, 8, PROWS).transpose(0, 2, 1)
    table = by_source.reshape(2, 64)
    mine = by_source % PROWS == row_here
    slots = jnp.sum(jnp.where(mine, by_source // PROWS, 0), axis=2)
    padded = pl.cdiv(count, GROUP) * GROUP
    hit = slots[:, :, None] == jnp.arange(padded)[None, None, :]
    which = jnp.max(jnp.where(hit, jnp.arange(16).reshape(2, 8, 1), -1), axis=1)
    front_parts = scatter_rows(blocks)
    first = jnp.concatenate([pieces, blocks[:2], jnp.zeros((6, BS, BS), jnp.float32)])
    got = lax.all_to_all(first.transpose(1, 0, 2), BOTH, 0, 0, tiled=True)
    onward, tops = route(col_map, table, got.reshape(PROWS, PCOLS, 24, BS))
    arrived = lax.all_to_all(onward.reshape(BS, 16, BS), BOTH, 0, 0, tiled=True)
    arrived = arrived.transpose(1, 0, 2)
    child_parts = scatter_rows(arrived)
    chunk = assemble(slots.reshape(16), front_parts, child_parts)
    panel = lax.all_gather(chunk, "pcol")
    known = lax.all_to_all(tops.reshape(BS, 16, BS), BOTH, 0, 0, tiled=True)
    weight, top = cholesky(place, known)
    result = update(place, which, weight, top, arrived, panel, blocks)
    return result.reshape(front.shape)


def solution(mesh):
    return jax.shard_map(
        on_device,
        mesh=mesh,
        in_specs=(
            P(None, "prow", None, None, "pcol", None),
            P(None, None, "prow", None, "pcol", None),
            P(),
            P(),
        ),
        out_specs=P(None, "prow", None, None, "pcol", None),
        check_vma=False,
    )
```

time: 769 us -> 261 us (0.34)
  waiting for transfers between devices: 511 us -> 141 us
  other arithmetic: 124 us -> 6.25 us
  Pallas kernels: 0 us -> 51.5 us
  matrix products: 49 us -> 0 us
  starting transfers between devices: 0.75 us -> 40.6 us
  local copies, waits for them, and re-layouts: 39.2 us -> 6.91 us
  blocking collectives: 20.4 us -> 0 us
    psum x4 -> x0, waiting for transfers between devices: 389 us -> none  [the longest x2 269 us: broadcast(): return lax.psum(block, axis)]
    another operation x18 -> x1, other arithmetic: 108 us -> 0.08 us  [on_device(): place = jnp.stack([row_here, col_here]).astype(jnp.int32)]
    all_gather x1, waiting for transfers between devices: 122 us -> 55.2 us  [on_device(): panel = lax.all_gather(chunk, 'pcol')]
    pallas_call x0 -> x4, Pallas kernels: none -> 51.5 us  [the longest x1 29.8 us: cholesky(): pl.pallas_call(functools.partial(cholesky_kernel, 16), out_shape=(jax.Sha...]
    all_to_all x0 -> x3, waiting for transfers between devices: none -> 49.1 us  [the longest x1 24.2 us: on_device(): got = lax.all_to_all(first.transpose(1, 0, 2), BOTH, 0, 0, tiled=True)]
    dot_general x8 -> x0, matrix products: 46.3 us -> none  [the longest x2 18.1 us: on_device(): change = jnp.dot(factor, col_factor.T, precision=HIGHEST_PRECISION)]
    ppermute x0 -> x6, waiting for transfers between devices: none -> 36.6 us  [scatter_rows(): parts.append(lax.ppermute(blocks[:, y * SUB:(y + 1) * SUB], 'pcol', pairs))]
    unnamed x26 -> x6, local copies, waits for them, and re-layouts: 28.4 us -> 2.1 us
  transfers between devices with their start and end apart: 5 -> 10, of which waited for: 5 -> 8; matrix products, arithmetic and copies ran while one was open for 0% -> 3% of each run, Pallas kernels for 0% -> 11%
where the time goes in v1:
time: 261 us; the launch traced here: 260 us
  waiting for transfers between devices  141 us (54%)
  Pallas kernels  51.5 us (20%)
  starting transfers between devices  40.6 us (16%)
  between operations  13.5 us (5%)
  local copies, waits for them, and re-layouts  6.91 us (3%)
  other arithmetic  6.25 us (2%)
    all_gather x1, waiting for transfers between devices, on_device(): panel = lax.all_gather(chunk, 'pcol')  55.2 us
    ppermute x6, waiting for transfers between devices, scatter_rows(): parts.append(lax.ppermute(blocks[:, y * SUB:(y + 1) * SUB], 'pcol', pairs))  36.6 us
    pallas_call x1, Pallas kernels, cholesky(): pl.pallas_call(functools.partial(cholesky_kernel, 16), out_shape=(jax.Sha...  29.8 us
    all_to_all x1, waiting for transfers between devices, on_device(): got = lax.all_to_all(first.transpose(1, 0, 2), BOTH, 0, 0, tiled=True)  24.2 us
    all_to_all x1, waiting for transfers between devices, on_device(): known = lax.all_to_all(tops.reshape(BS, 16, BS), BOTH, 0, 0, tiled=True)  18.8 us
    pallas_call x1, Pallas kernels, update(): pl.pallas_call(update_kernel, out_shape=jax.ShapeDtypeStruct(front.shape,...  15.9 us
    ppermute x6, starting transfers between devices, scatter_rows(): parts.append(lax.ppermute(blocks[:, y * SUB:(y + 1) * SUB], 'pcol', pairs))  14.8 us
    all_to_all x1, starting transfers between devices, on_device(): got = lax.all_to_all(first.transpose(1, 0, 2), BOTH, 0, 0, tiled=True)  11.1 us
  transfers between devices with their start and end apart: 10, of which 8 were waited for; matrix products, arithmetic and copies ran while one was open for 3% of the time, Pallas kernels for 11%

profile of v1, /device:TPU:0, one launch (start us, length us, event | category | flops | bytes accessed | tf_op | source)
XLA Modules:
  0.0 259.7 jit_solution(14536066536377283973)
XLA Ops:
  6.5 0.9 slice.30
  7.5 0.1 copy.17
  7.6 1.8 copy.16
  9.4 0.1 pad.2.clone
  9.5 1.3 maximum_bitcast_fusion
  10.8 0.0 copy-start.2
  10.8 0.0 copy-start.1
  10.8 11.1 %all-to-all-start = ((f32[128,24,128]{2,1,0:T(8,128)}), f32[128,24,128]{2,1,0:T(8,128)S(1)}, u32[]{:S(2)}, u32[]{:S(2)}) async-start(f32[128,24,128]{2,1,0:T(8,128)} %maximum_bitcast_fusion), calls=%async_computation | async-start | bytes 3145728 | tf_op jit(solution)/shard_map/all_to_all | solution.py:289
  22.0 0.0 copy-done.2
  22.0 0.1 reshape.46
  22.1 0.1 copy.15
  22.1 0.1 reshape.50.table_ref
  22.2 24.2 %all-to-all-done = f32[128,24,128]{2,1,0:T(8,128)S(1)} async-done(((f32[128,24,128]{2,1,0:T(8,128)}), f32[128,24,128]{2,1,0:T(8,128)S(1)}, u32[]{:S(2)}, u32[]{:S(2)}) %all-to-all-start) | async-done | bytes 1572896 | tf_op jit(solution)/shard_map/all_to_all | solution.py:289
  46.4 0.0 copy-done.1
  46.4 2.9 %route.1 = (f32[8,16,16,128]{3,2,1,0:T(8,128)}, f32[8,16,16,128]{3,2,1,0:T(8,128)}) custom-call(s32[2,16]{1,0:T(2,128)S(1)} %copy-done.1, s32[2,64]{1,0:T(2,128)S(1)} %reshape.50.table_ref, f32[8,16,24,128]{3,2,1,0:T(8,128)S(1)} %bitcast.23), custom_call_target="tpu_custom_call" | custom-call | tf_op jit(solution)/shard_map/route/pallas_call | solution.py:76
  49.4 5.8 %all-to-all-start.2 = ((f32[128,16,128]{2,1,0:T(8,128)}), f32[128,16,128]{2,1,0:T(8,128)}, u32[]{:S(2)}, u32[]{:S(2)}) async-start(f32[128,16,128]{2,1,0:T(8,128)} %bitcast.8), calls=%async_computation.2 | async-start | bytes 2097152 | tf_op jit(solution)/shard_map/all_to_all | solution.py:291
  55.1 0.0 all-gather.3.cloned.1.call-start
  55.2 3.8 %fusion.5 = (f32[59,32,128]{2,1,0:T(8,128)}, f32[59,32,128]{2,1,0:T(8,128)}, f32[59,32,128]{2,1,0:T(8,128)}, f32[59,32,128]{2,1,0:T(8,128)S(1)}) fusion(f32[59,128,128]{2,1,0:T(8,128)} %bitcast.19, pred[]{:T(512)S(6)} %lt.11), kind=kLoop, calls=%fused_computation.19 | loop fusion | flops 241664 | bytes 7733249 | tf_op jit(solution)/shard_map/slice | solution.py:269
  59.0 4.1 %collective-permute-start.2 = (f32[59,32,128]{2,1,0:T(8,128)}, f32[59,32,128]{2,1,0:T(8,128)S(1)}, u32[]{:S(2)}, u32[]{:S(2)}) collective-permute-start(f32[59,32,128]{2,1,0:T(8,128)} %get-tuple-element.13), channel_id=1, source_target_pairs={{0,12},{1,13},{2,14},{3,15},{16,28},{17,29},{18,30},{19,31},{32,44... | collective-permute-start | bytes 2899976 | tf_op jit(solution)/shard_map/ppermute | solution.py:269
  63.1 2.3 collective-permute-start.1
  65.4 2.3 collective-permute-start
  67.6 6.1 %all-to-all-done.2 = f32[128,16,128]{2,1,0:T(8,128)} async-done(((f32[128,16,128]{2,1,0:T(8,128)}), f32[128,16,128]{2,1,0:T(8,128)}, u32[]{:S(2)}, u32[]{:S(2)}) %all-to-all-start.2) | async-done | bytes 1048608 | tf_op jit(solution)/shard_map/all_to_all | solution.py:291
  73.7 1.6 copy.21
  75.3 0.9 fusion.6
  76.2 2.2 collective-permute-start.5
  78.4 2.0 collective-permute-start.4
  80.4 6.9 %collective-permute-done.2.f3 = f32[59,32,128]{2,1,0:T(8,128)S(1)} collective-permute-done((f32[59,32,128]{2,1,0:T(8,128)}, f32[59,32,128]{2,1,0:T(8,128)S(1)}, u32[]{:S(2)}, u32[]{:S(2)}) %collective-permute-start.2) | collective-permute-done | bytes 966688 | tf_op jit(solution)/shard_map/ppermute | solution.py:269
  87.4 2.0 collective-permute-start.3
  89.4 0.1 reshape.55.slot_ref
  89.4 0.0 collective-permute-done.1.f2
  89.4 18.6 %collective-permute-done.f1 = f32[59,32,128]{2,1,0:T(8,128)} collective-permute-done((f32[59,32,128]{2,1,0:T(8,128)}, f32[59,32,128]{2,1,0:T(8,128)}, u32[]{:S(2)}, u32[]{:S(2)}) %collective-permute-start) | collective-permute-done | bytes 966688 | tf_op jit(solution)/shard_map/ppermute | solution.py:269
  108.1 0.0 collective-permute-done.5.c3
  108.1 5.6 %collective-permute-done.4.c2 = f32[16,32,128]{2,1,0:T(8,128)} collective-permute-done((f32[16,32,128]{2,1,0:T(8,128)}, f32[16,32,128]{2,1,0:T(8,128)}, u32[]{:S(2)}, u32[]{:S(2)}) %collective-permute-start.4) | collective-permute-done | bytes 262176 | tf_op jit(solution)/shard_map/ppermute | solution.py:269
  113.7 5.5 %collective-permute-done.3.c1 = f32[16,32,128]{2,1,0:T(8,128)} collective-permute-done((f32[16,32,128]{2,1,0:T(8,128)}, f32[16,32,128]{2,1,0:T(8,128)}, u32[]{:S(2)}, u32[]{:S(2)}) %collective-permute-start.3) | collective-permute-done | bytes 262176 | tf_op jit(solution)/shard_map/ppermute | solution.py:269
  119.1 2.9 %assemble.1 = f32[59,32,128]{2,1,0:T(8,128)} custom-call(s32[16]{0:T(128)S(1)} %reshape.55.slot_ref, f32[59,32,128]{2,1,0:T(8,128)S(1)} %get-tuple-element.16.f0, f32[59,32,128]{2,1,0:T(8,128)} %collective-permute-done.f1, f32[59,32,128]{2,1,0:T(8,128)} %collective-permute-done.1.f2, f32[59,32,128]{2,1,0:T(8,128)S(1)} %collective-permute-done.2.f3, ...), custom_call_target="tpu_custom_call" | custom-call | tf_op jit(solution)/shard_map/assemble/pallas_call | solution.py:192
  122.0 0.0 all-gather.3.cloned.1.call-update
  122.1 8.8 %all-to-all-start.1 = ((f32[128,16,128]{2,1,0:T(8,128)}), f32[128,16,128]{2,1,0:T(8,128)S(1)}, u32[]{:S(2)}, u32[]{:S(2)}) async-start(f32[128,16,128]{2,1,0:T(8,128)} %bitcast.7), calls=%async_computation.1 | async-start | bytes 2097152 | tf_op jit(solution)/shard_map/all_to_all | solution.py:296
  130.9 0.1 pad_add_fusion.place_ref
  131.0 0.1 select_reduce_fusion.which_ref
  131.1 18.8 %all-to-all-done.1.got_ref = f32[128,16,128]{2,1,0:T(8,128)S(1)} async-done(((f32[128,16,128]{2,1,0:T(8,128)}), f32[128,16,128]{2,1,0:T(8,128)S(1)}, u32[]{:S(2)}, u32[]{:S(2)}) %all-to-all-start.1) | async-done | bytes 1048608 | tf_op jit(solution)/shard_map/all_to_all | solution.py:296
  149.9 29.8 %cholesky.1 = (f32[512,128]{1,0:T(8,128)S(1)}, f32[128,128]{1,0:T(8,128)S(1)}) custom-call(s32[2]{0:T(128)S(1)} %pad_add_fusion.place_ref, f32[128,16,128]{2,1,0:T(8,128)S(1)} %all-to-all-done.1.got_ref), custom_call_target="tpu_custom_call" | custom-call | tf_op jit(solution)/shard_map/cholesky/pallas_call | solution.py:164
  179.7 55.2 %all-gather.3.cloned.1.call-done = f32[944,32,128]{2,1,0:T(8,128)} async-done(((f32[59,32,128]{2,1,0:T(8,128)}), f32[944,32,128]{2,1,0:T(8,128)}) %all-gather.3.cloned.1.call-update) | async-done | bytes 15466512 | tf_op jit(solution)/shard_map/all_gather | solution.py:295
  234.8 0.0 copy-start
  234.8 2.1 copy-done
  236.9 15.9 %update.1 = f32[59,128,128]{2,1,0:T(8,128)} custom-call(s32[2]{0:T(128)S(1)} %pad_add_fusion.place_ref, s32[2,60]{1,0:T(2,128)S(1)} %select_reduce_fusion.which_ref, f32[512,128]{1,0:T(8,128)S(1)} %get-tuple-element.10.weight_ref, f32[128,128]{1,0:T(8,128)S(1)} %get-tuple-element.11.top_ref, f32[16,128,128]{2,1,0:T(8,128)S(1)} %bitcast.22, ...), custom_call_target="tpu_custom_call" | custom-call | tf_op jit(solution)/shard_map/update/pallas_call | solution.py:241
  (3 shorter events, 0.0 us)
Async XLA Ops:
  10.8 11.2 %copy-start.2 = (s32[2,64]{1,0:T(2,128)S(1)}, s32[2,64]{1,0:T(2,128)}, u32[]{:S(2)}) copy-start(s32[2,64]{1,0:T(2,128)} %param.6) | copy-start | bytes 1540
  10.8 35.6 %copy-start.1 = (s32[2,16]{1,0:T(2,128)S(1)}, s32[2,16]{1,0:T(2,128)}, u32[]{:S(2)}) copy-start(s32[2,16]{1,0:T(2,128)} %col_ref.1) | copy-start | bytes 388
  10.8 35.6 %all-to-all-start = ((f32[128,24,128]{2,1,0:T(8,128)}), f32[128,24,128]{2,1,0:T(8,128)S(1)}, u32[]{:S(2)}, u32[]{:S(2)}) async-start(f32[128,24,128]{2,1,0:T(8,128)} %maximum_bitcast_fusion), calls=%async_computation | async-start | bytes 3145728 | tf_op jit(solution)/shard_map/all_to_all | solution.py:289
  49.4 24.4 %all-to-all-start.2 = ((f32[128,16,128]{2,1,0:T(8,128)}), f32[128,16,128]{2,1,0:T(8,128)}, u32[]{:S(2)}, u32[]{:S(2)}) async-start(f32[128,16,128]{2,1,0:T(8,128)} %bitcast.8), calls=%async_computation.2 | async-start | bytes 2097152 | tf_op jit(solution)/shard_map/all_to_all | solution.py:291
  55.1 179.7 %all-gather.3.cloned.1.call-start = ((), (), s32[]{:S(2)}) async-start(), calls=%async_computation.3 | async-start | bytes 16433152 | tf_op jit(solution)/shard_map/all_gather | solution.py:295
  59.0 28.4 %collective-permute-start.2 = (f32[59,32,128]{2,1,0:T(8,128)}, f32[59,32,128]{2,1,0:T(8,128)S(1)}, u32[]{:S(2)}, u32[]{:S(2)}) collective-permute-start(f32[59,32,128]{2,1,0:T(8,128)} %get-tuple-element.13), channel_id=1, source_target_pairs={{0,12},{1,13},{2,14},{3,15},{16,28},{17,29},{18,30},{19,31},{32,44... | collective-permute-start | bytes 2899976 | tf_op jit(solution)/shard_map/ppermute | solution.py:269
  63.1 26.3 %collective-permute-start.1 = (f32[59,32,128]{2,1,0:T(8,128)}, f32[59,32,128]{2,1,0:T(8,128)}, u32[]{:S(2)}, u32[]{:S(2)}) collective-permute-start(f32[59,32,128]{2,1,0:T(8,128)} %get-tuple-element.14), channel_id=1, source_target_pairs={{0,8},{1,9},{2,10},{3,11},{16,24},{17,25},{18,26},{19,27},{32,40},... | collective-permute-start | bytes 2899976 | tf_op jit(solution)/shard_map/ppermute | solution.py:269
  65.4 42.7 %collective-permute-start = (f32[59,32,128]{2,1,0:T(8,128)}, f32[59,32,128]{2,1,0:T(8,128)}, u32[]{:S(2)}, u32[]{:S(2)}) collective-permute-start(f32[59,32,128]{2,1,0:T(8,128)} %get-tuple-element.15), channel_id=1, source_target_pairs={{0,4},{1,5},{2,6},{3,7},{16,20},{17,21},{18,22},{19,23},{32,36},{3... | collective-permute-start | bytes 2899976 | tf_op jit(solution)/shard_map/ppermute | solution.py:269
  76.2 31.9 %collective-permute-start.5 = (f32[16,32,128]{2,1,0:T(8,128)}, f32[16,32,128]{2,1,0:T(8,128)S(1)}, u32[]{:S(2)}, u32[]{:S(2)}) collective-permute-start(f32[16,32,128]{2,1,0:T(8,128)} %get-tuple-element.17), channel_id=1, source_target_pairs={{0,12},{1,13},{2,14},{3,15},{16,28},{17,29},{18,30},{19,31},{32,44... | collective-permute-start | bytes 786440 | tf_op jit(solution)/shard_map/ppermute | solution.py:269
  78.4 35.3 %collective-permute-start.4 = (f32[16,32,128]{2,1,0:T(8,128)}, f32[16,32,128]{2,1,0:T(8,128)}, u32[]{:S(2)}, u32[]{:S(2)}) collective-permute-start(f32[16,32,128]{2,1,0:T(8,128)} %get-tuple-element.18), channel_id=1, source_target_pairs={{0,8},{1,9},{2,10},{3,11},{16,24},{17,25},{18,26},{19,27},{32,40},... | collective-permute-start | bytes 786440 | tf_op jit(solution)/shard_map/ppermute | solution.py:269
  87.4 31.8 %collective-permute-start.3 = (f32[16,32,128]{2,1,0:T(8,128)}, f32[16,32,128]{2,1,0:T(8,128)}, u32[]{:S(2)}, u32[]{:S(2)}) collective-permute-start(f32[16,32,128]{2,1,0:T(8,128)} %get-tuple-element.19), channel_id=1, source_target_pairs={{0,4},{1,5},{2,6},{3,7},{16,20},{17,21},{18,22},{19,23},{32,36},{3... | collective-permute-start | bytes 786440 | tf_op jit(solution)/shard_map/ppermute | solution.py:269
  122.1 27.8 %all-to-all-start.1 = ((f32[128,16,128]{2,1,0:T(8,128)}), f32[128,16,128]{2,1,0:T(8,128)S(1)}, u32[]{:S(2)}, u32[]{:S(2)}) async-start(f32[128,16,128]{2,1,0:T(8,128)} %bitcast.7), calls=%async_computation.1 | async-start | bytes 2097152 | tf_op jit(solution)/shard_map/all_to_all | solution.py:296
  234.8 2.1 copy-start
Sparse Core Ops, SparseCore 0:
  122.2 112.6 all-gather.2
